TPU v7x, 32 devices: a whole 2x2x4 slice. The times are simulated.
32 devices in a mesh: rep: 8 (over y, x, core), exp: 4 (over z).
Axes of the slice: x: 2, y: 2, z: 4, core: 2. Of those that a mesh axis runs over, the one named last changes fastest.
Arguments:
- hidden: bfloat16 [4096, 4096], P(('rep', 'exp')), may hold values from -6 to 6
- parents: int32 [4096], P(('rep', 'exp')), may hold values from 0 to 511
- routes: int32 [4096, 8], P(('rep', 'exp')), may hold values from 0 to 31, all different within a row; in each aligned block of 128 rows (0 to 127, 128 to 255, ...) at most 34 rows name the same one
- gates: float32 [4096, 8], P(('rep', 'exp')), may hold values from 0.05 to 1
- counts: int32 [32], P(('rep', 'exp')), may hold values from 64 to 128, as said below
- norm_gain: float32 [4096], replicated, may hold values from 0.1 to 1.9
- w_gate: bfloat16 [32, 4096, 768], P(('rep', 'exp')), may hold values from -0.09375 to 0.09375
- w_up: bfloat16 [32, 4096, 768], P(('rep', 'exp')), may hold values from -0.09375 to 0.09375
- w_down: bfloat16 [32, 768, 4096], P(('rep', 'exp')), may hold values from -0.21875 to 0.21875
Outputs:
- mixed: bfloat16 [4096, 4096], P(('rep', 'exp'))
Inputs may be any that keep to these rules, and one draw needn't show every extreme that they name: `routes`: in the rows of one device no expert is named more than 34 times. `counts`: some device has all of its rows live.
All inputs are finite; a program needn't handle non-finite values.
Results may differ from a plain program's by a relative error of at most 0.0071.
Values may be sent and summed in bfloat16 or wider, within the bound.
No kernel may reach another device: no remote copies, remote signals or barrier semaphores. Data moves between devices by JAX's collectives and lax.ppermute only.
A program may use at most 128 MiB of HBM per device.

v0:
```python
import jax
import jax.numpy as jnp
from jax import lax
from jax.sharding import PartitionSpec as P


def run_expert(arrived, w_gate, w_up, w_down):
    gate_val = jnp.dot(arrived, w_gate[0], preferred_element_type=jnp.float32)
    up_val = jnp.dot(arrived, w_up[0], preferred_element_type=jnp.float32)
    act = (jax.nn.silu(gate_val) * up_val).astype(jnp.bfloat16)
    return jnp.dot(act, w_down[0], preferred_element_type=jnp.float32).astype(jnp.bfloat16)


def shards(hidden, parents, routes, gates, counts, norm_gain, w_gate, w_up, w_down):
    rows = hidden.shape[0]
    width = hidden.shape[1]
    top = routes.shape[1]
    n_rep = lax.axis_size("rep")
    n_exp = lax.axis_size("exp")
    n_dev = n_rep * n_exp
    cap = rows * top // n_dev + 2
    group = lax.all_gather(hidden, "exp", axis=0, tiled=True)
    picked = jnp.take(group, parents, axis=0).astype(jnp.float32)
    scale = lax.rsqrt(jnp.mean(picked * picked, axis=1, keepdims=True) + 1e-06)
    normed = (picked * scale * norm_gain).astype(jnp.bfloat16)
    live = jnp.arange(rows, dtype=jnp.int32) < counts[0]
    weights = gates / jnp.sum(gates, axis=1, keepdims=True) * live[:, None].astype(jnp.float32)
    flat = routes.reshape(-1)
    live_slot = jnp.repeat(live, top)
    onehot = (
        (flat[:, None] == jnp.arange(n_dev, dtype=jnp.int32)[None, :]) & live_slot[:, None]
    ).astype(jnp.int32)
    before = jnp.cumsum(onehot, axis=0) - onehot
    rank = jnp.sum(before * onehot, axis=1)
    position = jnp.where(live_slot, flat * cap + rank, n_dev * cap)
    row_of_slot = jnp.arange(rows * top, dtype=jnp.int32) // top
    source = jnp.zeros((n_dev * cap,), jnp.int32).at[position].set(row_of_slot, mode="drop")
    filled = jnp.zeros((n_dev * cap,), jnp.bool_).at[position].set(True, mode="drop")
    outgoing = jnp.where(
        filled[:, None], jnp.take(normed, source, axis=0), jnp.zeros((), jnp.bfloat16)
    )
    arrived = lax.all_to_all(outgoing, ("rep", "exp"), split_axis=0, concat_axis=0, tiled=True)
    results = run_expert(arrived, w_gate, w_up, w_down)
    returned = lax.all_to_all(results, ("rep", "exp"), split_axis=0, concat_axis=0, tiled=True)
    safe = jnp.minimum(position, n_dev * cap - 1)
    collected = jnp.take(returned, safe, axis=0).reshape(rows, top, width)
    mixed = jnp.zeros((rows, width), jnp.float32)
    for slot in range(top):
        mixed = mixed + weights[:, slot : slot + 1] * collected[:, slot].astype(jnp.float32)
    return mixed.astype(jnp.bfloat16)


def solution(mesh):
    placed = (
        P(("rep", "exp"), None),
        P(("rep", "exp")),
        P(("rep", "exp"), None),
        P(("rep", "exp"), None),
        P(("rep", "exp")),
        P(),
        P(("rep", "exp"), None, None),
        P(("rep", "exp"), None, None),
        P(("rep", "exp"), None, None),
    )
    return jax.shard_map(
        shards, mesh=mesh, in_specs=placed, out_specs=P(("rep", "exp"), None), check_vma=False
    )
```

profile of v0, /device:TPU:0, one launch (start us, length us, event | category | flops | bytes accessed | tf_op | source)
XLA Modules:
  0.0 702.0 jit_solution(11272931611687938119)
XLA Ops:
  6.5 0.7 all-gather.2.cloned.1.call-update
  8.0 0.1 reshape.171
  8.1 0.1 reshape.173
  8.2 0.8 copy.18
  9.4 0.7 broadcast_multiply_fusion
  10.3 9.0 %reduce-window.6 = s32[32,8,128]{2,1,0:T(8,128)S(1)} reduce-window(s32[32,8,128]{2,1,0:T(8,128)S(1)} %fusion.27, s32[]{:T(128)} %constant.73.clone.1), window={size=1x1x128 pad=0_0x0_0x127_0}, to_apply=%region_1.2 | reduce-window | flops 4161536 | bytes 262148 | tf_op jit(solution)/shard_map/reduce-window
  19.4 0.1 copy.21
  19.9 4.3 scatter_custom_fusion.1
  24.2 0.1 broadcast_in_dim.91
  24.3 4.3 scatter_custom_fusion
  28.7 0.1 broadcast_in_dim.88
  28.8 0.7 compare_select_fusion.4
  29.5 0.7 compare_and_fusion.2
  30.1 62.3 %all-gather.2.cloned.1.call-done = bf16[512,4096]{1,0:T(8,128)(2,1)} async-done(((bf16[128,4096]{1,0:T(8,128)(2,1)}), bf16[512,4096]{1,0:T(8,128)(2,1)}) %all-gather.2.cloned.1.call-update) | async-done | bytes 4194320 | tf_op jit(solution)/shard_map/all_gather | solution.py:22
  92.5 4.9 gather_fusion
  97.4 0.4 fusion.11
  97.9 0.4 fusion.13
  98.3 7.7 %gather_fusion.1 = bf16[1088,4096]{1,0:T(8,128)(2,1)} fusion(bf16[128,4096]{1,0:T(8,128)(2,1)S(1)} %fusion.13, s32[2048]{0:T(1024)S(1)} %pad_clamp_fusion), kind=kCustom, calls=%fused_computation.1 | custom fusion | bytes 17830144 | tf_op jit(solution)/shard_map/jit(_take)/gather | solution.py:40
  106.0 10.3 %gather.18 = bf16[32,34,4096]{2,1,0:T(8,128)(2,1)} reshape(bf16[1088,4096]{1,0:T(8,128)(2,1)} %gather_fusion.1) | data formatting | bytes 17825792 | tf_op jit(solution)/shard_map/jit(_take)/gather | solution.py:40
  116.3 6.0 select_select_fusion
  122.3 230.6 %all_to_all.21 = bf16[32,34,4096]{2,1,0:T(8,128)(2,1)} all-to-all(bf16[32,34,4096]{2,1,0:T(8,128)(2,1)S(1)} %select_select_fusion), channel_id=1, replica_groups=mesh['rep'=8,'exp'=4] {'rep','exp'}, dimensions={0} | all-to-all | bytes 17825792 | tf_op jit(solution)/shard_map/all_to_all | solution.py:42
  352.8 10.6 %all_to_all.15 = bf16[1088,4096]{1,0:T(8,128)(2,1)} reshape(bf16[32,34,4096]{2,1,0:T(8,128)(2,1)} %all_to_all.21) | data formatting | bytes 17825792 | tf_op jit(solution)/shard_map/all_to_all | solution.py:42
  363.4 11.5 %fusion.3 = f32[1088,768]{1,0:T(8,128)S(1)} fusion(bf16[1088,4096]{1,0:T(8,128)(2,1)} %all_to_all.15, bf16[1,4096,768]{2,1,0:T(8,128)(2,1)} %param.15), kind=kOutput, calls=%fused_computation.11 | convolution fusion | flops 6845104128 | bytes 18546688 | tf_op jit(solution)/shard_map/dot_general | solution.py:8
  375.0 7.5 %fusion.8 = bf16[1088,768]{1,0:T(8,128)(2,1)S(1)} fusion(bf16[1088,4096]{1,0:T(8,128)(2,1)S(1)} %copy-done, bf16[1,4096,768]{2,1,0:T(8,128)(2,1)S(1)} %bitcast.107, f32[1088,768]{1,0:T(8,128)S(1)} %fusion.3), kind=kOutput, calls=%fused_computation.14 | convolution fusion | flops 6850117632 | bytes 20217856 | tf_op jit(solution)/shard_map/dot_general | solution.py:9
  382.6 9.4 %convolution_convert_fusion = bf16[1088,4096]{1,0:T(8,128)(2,1)} fusion(bf16[1088,768]{1,0:T(8,128)(2,1)S(1)} %fusion.8, bf16[1,768,4096]{2,1,0:T(8,128)(2,1)S(1)} %bitcast.109), kind=kOutput, calls=%fused_computation.5 | convolution fusion | flops 6849560576 | bytes 16875520 | tf_op jit(solution)/shard_map/dot_general | solution.py:11
  392.0 10.3 %all_to_all.16 = bf16[32,34,4096]{2,1,0:T(8,128)(2,1)} reshape(bf16[1088,4096]{1,0:T(8,128)(2,1)} %convolution_convert_fusion) | data formatting | bytes 17825792 | tf_op jit(solution)/shard_map/all_to_all | solution.py:44
  402.3 14.6 %all-to-all-start.1 = ((bf16[32,34,4096]{2,1,0:T(8,128)(2,1)}), bf16[32,34,4096]{2,1,0:T(8,128)(2,1)}, u32[]{:S(2)}, u32[]{:S(2)}) async-start(bf16[32,34,4096]{2,1,0:T(8,128)(2,1)} %all_to_all.16), calls=%async_computation.1 | async-start | bytes 20971520 | tf_op jit(solution)/shard_map/all_to_all | solution.py:44
  417.2 226.0 %all-to-all-done.1 = bf16[32,34,4096]{2,1,0:T(8,128)(2,1)} async-done(((bf16[32,34,4096]{2,1,0:T(8,128)(2,1)}), bf16[32,34,4096]{2,1,0:T(8,128)(2,1)}, u32[]{:S(2)}, u32[]{:S(2)}) %all-to-all-start.1) | async-done | bytes 8912928 | tf_op jit(solution)/shard_map/all_to_all | solution.py:44
  643.2 10.4 %all_to_all.18 = bf16[1088,4096]{1,0:T(8,128)(2,1)} reshape(bf16[32,34,4096]{2,1,0:T(8,128)(2,1)} %all-to-all-done.1) | data formatting | bytes 17825792 | tf_op jit(solution)/shard_map/all_to_all | solution.py:44
  653.7 19.8 %gather_fusion.2 = bf16[1024,4096]{1,0:T(8,128)(2,1)} fusion(bf16[1088,4096]{1,0:T(8,128)(2,1)} %all_to_all.18, s32[1024]{0:T(1024)S(1)} %broadcast_clamp_fusion), kind=kCustom, calls=%fused_computation.2 | custom fusion | bytes 16781312 | tf_op jit(solution)/shard_map/jit(_take)/gather | solution.py:46
  673.4 16.3 %copy_select_fusion = bf16[128,8,4096]{2,0,1:T(8,128)(2,1)} fusion(bf16[128,8,4096]{2,1,0:T(8,128)(2,1)} %bitcast.99, pred[128,8]{0,1:T(8,128)(4,1)S(1)} %compare_and_fusion.1), kind=kLoop, calls=%fused_computation.7 | loop fusion | flops 4194304 | bytes 16778240 | tf_op jit(solution)/shard_map/jit(_take)/select_n | solution.py:46
  689.8 5.3 fusion.15
  (50 shorter events, 1.3 us)
Async XLA Ops:
  6.5 85.9 %all-gather.2.cloned.1.call-start = ((), (), s32[]{:S(2)}) async-start(), calls=%async_computation.2 | async-start | bytes 5242880 | tf_op jit(solution)/shard_map/all_gather | solution.py:22
  30.1 67.7 %copy-start.2 = (f32[4096]{0:T(1024)S(1)}, f32[4096]{0:T(1024)}, u32[]{:S(2)}) copy-start(f32[4096]{0:T(1024)} %param.14) | copy-start | bytes 49156
  352.8 22.1 %slice-start = ((s8[6291456]{0:T(1024)(128)(4,1)}), s8[2097152]{0:T(1024)(128)(4,1)S(1)}, s32[]{:S(2)}) async-start(s8[6291456]{0:T(1024)(128)(4,1)} %bitcast.106), calls=%async_computation.3 | async-start | bytes 4194304
  363.4 11.6 %copy-start = (bf16[1088,4096]{1,0:T(8,128)(2,1)S(1)}, bf16[1088,4096]{1,0:T(8,128)(2,1)}, u32[]{:S(2)}) copy-start(bf16[1088,4096]{1,0:T(8,128)(2,1)} %all_to_all.15) | copy-start | bytes 26738692
  363.4 11.6 %slice-start.1 = ((s8[6291456]{0:T(1024)(128)(4,1)}), s8[4194304]{0:T(1024)(128)(4,1)S(1)}, s32[]{:S(2)}) async-start(s8[6291456]{0:T(1024)(128)(4,1)} %bitcast.106), calls=%async_computation.4 | async-start | bytes 8388608
  363.4 19.1 %slice-start.2 = ((s8[6291456]{0:T(1024)(128)(4,1)}), s8[4194304]{0:T(1024)(128)(4,1)S(1)}, s32[]{:S(2)}) async-start(s8[6291456]{0:T(1024)(128)(4,1)} %bitcast.108), calls=%async_computation.5 | async-start | bytes 8388608
  375.0 7.6 %slice-start.3 = ((s8[6291456]{0:T(1024)(128)(4,1)}), s8[2097152]{0:T(1024)(128)(4,1)S(1)}, s32[]{:S(2)}) async-start(s8[6291456]{0:T(1024)(128)(4,1)} %bitcast.108), calls=%async_computation.6 | async-start | bytes 4194304
  402.3 14.8 %copy-start.3 = (f32[128,8]{0,1:T(8,128)S(1)}, f32[128,8]{0,1:T(8,128)}, u32[]{:S(2)}) copy-start(f32[128,8]{0,1:T(8,128)} %param.12) | copy-start | bytes 12292
  402.3 14.8 %copy-start.1 = (s32[128,8]{0,1:T(8,128)S(1)}, s32[128,8]{0,1:T(8,128)}, u32[]{:S(2)}) copy-start(s32[128,8]{0,1:T(8,128)} %param.11) | copy-start | bytes 12292
  402.3 240.9 %all-to-all-start.1 = ((bf16[32,34,4096]{2,1,0:T(8,128)(2,1)}), bf16[32,34,4096]{2,1,0:T(8,128)(2,1)}, u32[]{:S(2)}, u32[]{:S(2)}) async-start(bf16[32,34,4096]{2,1,0:T(8,128)(2,1)} %all_to_all.16), calls=%async_computation.1 | async-start | bytes 20971520 | tf_op jit(solution)/shard_map/all_to_all | solution.py:44
Sparse Core Ops, SparseCore 0:
  8.9 83.5 all-gather.1
where the time goes:
time: 711 us; the launch traced here: 702 us
  waiting for transfers between devices  289 us (41%)
  blocking collectives  231 us (32%)
  local copies, waits for them, and re-layouts  85.1 us (12%)
  other arithmetic  39.7 us (6%)
  matrix products  28.5 us (4%)
  starting transfers between devices  14.6 us (2%)
  between operations  14.5 us (2%)
    all_to_all x1, blocking collectives, shards(): lax.all_to_all(outgoing, ('rep', 'exp'), split_axis=0, concat_axis=0, til...  231 us
    all_to_all x1, waiting for transfers between devices, shards(): lax.all_to_all(results, ('rep', 'exp'), split_axis=0, concat_axis=0, tile...  226 us
    all_gather x1, waiting for transfers between devices, shards(): group = lax.all_gather(hidden, 'exp', axis=0, tiled=True)  62.3 us
    all_to_all x2, local copies, waits for them, and re-layouts, shards(): lax.all_to_all(results, ('rep', 'exp'), split_axis=0, concat_axis=0, tile...  20.8 us
    gather x1, local copies, waits for them, and re-layouts, shards(): collected = jnp.take(returned, safe, axis=0).reshape(rows, top, width)  19.8 us
    gather x2, local copies, waits for them, and re-layouts, shards(): jnp.take(normed, source, axis=0)  18 us
    select_n x2, other arithmetic, shards(): collected = jnp.take(returned, safe, axis=0).reshape(rows, top, width)  16.4 us
    all_to_all x1, starting transfers between devices, shards(): lax.all_to_all(results, ('rep', 'exp'), split_axis=0, concat_axis=0, tile...  14.6 us
  transfers between devices with their start and end apart: 2, of which 2 were waited for; matrix products, arithmetic and copies ran while one was open for 3% of the time, Pallas kernels for 0%

commit v1 on v0

v1 whole, which is shorter than its diff:
```python
import jax
import jax.numpy as jnp
from jax import lax
from jax.sharding import PartitionSpec as P

IN_CHUNKS = 4
OUT_CHUNKS = 4


def dot(a, b):
    return jnp.dot(a, b, preferred_element_type=jnp.float32)


def exchange(blocks, n_rep, back):
    moved = [blocks[0]]
    for step in range(1, n_rep):
        shift = n_rep - step if back else step
        pairs = [(i, (i + shift) % n_rep) for i in range(n_rep)]
        moved.append(lax.ppermute(blocks[step], "rep", pairs))
    return moved


def shards(hidden, parents, routes, gates, counts, norm_gain, w_gate, w_up, w_down):
    rows, width = hidden.shape
    top = routes.shape[1]
    n_rep = lax.axis_size("rep")
    n_exp = lax.axis_size("exp")
    cap = (rows * top // (n_rep * n_exp) + 2) * n_exp
    group = rows * n_exp
    my_rep = lax.axis_index("rep")
    my_exp = lax.axis_index("exp")
    bf16 = jnp.bfloat16

    live = jnp.arange(rows, dtype=jnp.int32) < counts[0]
    weights = gates / jnp.sum(gates, axis=1, keepdims=True) * live[:, None].astype(jnp.float32)
    named = jnp.where(live[:, None], routes, -1)
    facts = jnp.concatenate(
        [named.astype(jnp.float32), parents[:, None].astype(jnp.float32), weights], axis=1
    )
    facts = lax.all_gather(facts, "exp", axis=0, tiled=True)

    value = hidden.astype(jnp.float32)
    scale = lax.rsqrt(jnp.mean(value * value, axis=1, keepdims=True) + 1e-06)
    normed = (value * scale * norm_gain).astype(bf16)

    named = facts[:, :top].astype(jnp.int32)
    parent = facts[:, top].astype(jnp.int32)
    weights = facts[:, top + 1 :]
    expert = (my_rep + jnp.arange(n_rep, dtype=jnp.int32)) % n_rep * n_exp + my_exp
    hit = named[:, :, None] == expert[None, None, :]
    match = jnp.any(hit, axis=1)
    share = jnp.sum(jnp.where(hit, weights[:, :, None], 0.0), axis=1)
    earlier = (
        jnp.arange(group, dtype=jnp.int32)[:, None] > jnp.arange(group, dtype=jnp.int32)[None, :]
    )
    rank = dot(earlier.astype(bf16), match.astype(bf16)).astype(jnp.int32)
    rank = jnp.where(match, rank, -1)
    slot = jnp.arange(cap, dtype=jnp.int32)
    taken = rank.T[:, None, :] == slot[None, :, None]
    of_parent = (parent[:, None] == jnp.arange(group, dtype=jnp.int32)[None, :]).astype(bf16)
    select = dot(taken.reshape(n_rep * cap, group).astype(bf16), of_parent).astype(bf16)
    mix = jnp.where(rank[:, :, None] == slot[None, None, :], share[:, :, None], 0.0)
    mix = mix.reshape(group, n_rep * cap)
    mix_high = mix.astype(bf16)
    mix_low = (mix - mix_high.astype(jnp.float32)).astype(bf16)

    step = width // IN_CHUNKS
    gate_val = 0.0
    up_val = 0.0
    for part in range(IN_CHUNKS):
        cols = slice(part * step, (part + 1) * step)
        held = lax.all_gather(normed[:, cols], "exp", axis=0, tiled=True)
        blocks = [
            dot(select[s * cap : (s + 1) * cap], held).astype(bf16) for s in range(n_rep)
        ]
        arrived = jnp.concatenate(exchange(blocks, n_rep, False), axis=0)
        gate_val = gate_val + dot(arrived, w_gate[0, cols])
        up_val = up_val + dot(arrived, w_up[0, cols])
    act = (jax.nn.silu(gate_val) * up_val).astype(bf16)

    step = width // OUT_CHUNKS
    mixed = []
    for part in range(OUT_CHUNKS):
        cols = slice(part * step, (part + 1) * step)
        result = dot(act, w_down[0, :, cols]).astype(bf16)
        blocks = [result[s * cap : (s + 1) * cap] for s in range(n_rep)]
        returned = jnp.concatenate(exchange(blocks, n_rep, True), axis=0)
        partial = (dot(mix_high, returned) + dot(mix_low, returned)).astype(bf16)
        mixed.append(lax.psum_scatter(partial, "exp", scatter_dimension=0, tiled=True))
    return jnp.concatenate(mixed, axis=1)


def solution(mesh):
    placed = (
        P(("rep", "exp"), None),
        P(("rep", "exp")),
        P(("rep", "exp"), None),
        P(("rep", "exp"), None),
        P(("rep", "exp")),
        P(),
        P(("rep", "exp"), None, None),
        P(("rep", "exp"), None, None),
        P(("rep", "exp"), None, None),
    )
    return jax.shard_map(
        shards, mesh=mesh, in_specs=placed, out_specs=P(("rep", "exp"), None), check_vma=False
    )
```

time: 711 us -> 429 us (0.60)
  blocking collectives: 231 us -> 15.1 us
  waiting for transfers between devices: 289 us -> 206 us
  local copies, waits for them, and re-layouts: 85.1 us -> 13.5 us
  matrix products: 28.5 us -> 92.2 us
  starting transfers between devices: 14.6 us -> 69.5 us
  other arithmetic: 39.7 us -> 7.52 us
    all_to_all x1 -> x0, blocking collectives: 231 us -> none  [shards(): lax.all_to_all(outgoing, ('rep', 'exp'), split_axis=0, concat_axis=0, til...]
    all_to_all x1 -> x0, waiting for transfers between devices: 226 us -> none  [shards(): lax.all_to_all(results, ('rep', 'exp'), split_axis=0, concat_axis=0, tile...]
    ppermute x0 -> x56, waiting for transfers between devices: none -> 115 us  [exchange(): moved.append(lax.ppermute(blocks[step], 'rep', pairs))]
    ppermute x0 -> x56, starting transfers between devices: none -> 69.2 us  [exchange(): moved.append(lax.ppermute(blocks[step], 'rep', pairs))]
    dot_general x3 -> x54, matrix products: 28.5 us -> 92.2 us  [dot(): return jnp.dot(a, b, preferred_element_type=jnp.float32)]
    gather x4 -> x0, local copies, waits for them, and re-layouts: 42.7 us -> none  [the longest x1 19.8 us: shards(): collected = jnp.take(returned, safe, axis=0).reshape(rows, top, width)]
    all_to_all x3 -> x0, local copies, waits for them, and re-layouts: 31.4 us -> none  [the longest x2 20.8 us: shards(): lax.all_to_all(results, ('rep', 'exp'), split_axis=0, concat_axis=0, tile...]
    reduce_scatter x0 -> x4, waiting for transfers between devices: none -> 26.8 us  [shards(): lax.psum_scatter(partial, 'exp', scatter_dimension=0, tiled=True)]
  transfers between devices with their start and end apart: 2 -> 64, of which waited for: 2 -> 32; matrix products, arithmetic and copies ran while one was open for 3% -> 21% of each run, Pallas kernels for 0% -> 0%
where the time goes in v1:
time: 429 us; the launch traced here: 420 us
  waiting for transfers between devices  206 us (48%)
  matrix products  92.2 us (21%)
  starting transfers between devices  69.5 us (16%)
  between operations  15.9 us (4%)
  blocking collectives  15.1 us (4%)
  local copies, waits for them, and re-layouts  13.5 us (3%)
  other arithmetic  7.52 us (2%)
    ppermute x56, waiting for transfers between devices, exchange(): moved.append(lax.ppermute(blocks[step], 'rep', pairs))  115 us
    dot_general x54, matrix products, dot(): return jnp.dot(a, b, preferred_element_type=jnp.float32)  92.2 us
    ppermute x56, starting transfers between devices, exchange(): moved.append(lax.ppermute(blocks[step], 'rep', pairs))  69.2 us
    all_gather x4, waiting for transfers between devices, shards(): held = lax.all_gather(normed[:, cols], 'exp', axis=0, tiled=True)  62.6 us
    reduce_scatter x4, waiting for transfers between devices, shards(): lax.psum_scatter(partial, 'exp', scatter_dimension=0, tiled=True)  26.8 us
    all_gather x1, blocking collectives, shards(): facts = lax.all_gather(facts, 'exp', axis=0, tiled=True)  15.1 us
    unnamed x120, local copies, waits for them, and re-layouts  8.77 us
  transfers between devices with their start and end apart: 64, of which 32 were waited for; matrix products, arithmetic and copies ran while one was open for 21% of the time, Pallas kernels for 0%

profile of v1, /device:TPU:0, one launch (start us, length us, event | category | flops | bytes accessed | tf_op | source)
XLA Modules:
  0.0 420.0 jit_solution(10374488758269766212)
XLA Ops:
  13.6 15.1 %all_gather.15 = f32[512,17]{0,1:T(8,128)S(1)} all-gather(f32[128,17]{0,1:T(8,128)S(1)} %pad_maximum_fusion.1), channel_id=1, replica_groups=mesh['rep'=8,'exp'=4] {'exp'}, dimensions={0}, use_global_device_ids=true | all-gather | bytes 43520 | tf_op jit(solution)/shard_map/all_gather | solution.py:40
  32.0 9.6 %all-gather.7.cloned.1.call-done = bf16[512,1024]{1,0:T(8,128)(2,1)} async-done(((bf16[128,1024]{1,0:T(8,128)(2,1)}), bf16[512,1024]{1,0:T(8,128)(2,1)}) %all-gather.7.cloned.1.call-update) | async-done | bytes 1048592 | tf_op jit(solution)/shard_map/all_gather | solution.py:72
  56.9 14.0 %all-gather.9.cloned.1.call-done = bf16[512,1024]{1,0:T(8,128)(2,1)} async-done(((bf16[128,1024]{1,0:T(8,128)(2,1)}), bf16[512,1024]{1,0:T(8,128)(2,1)}) %all-gather.9.cloned.1.call-update) | async-done | bytes 1048592 | tf_op jit(solution)/shard_map/all_gather | solution.py:72
  81.8 18.2 %all-gather.5.cloned.1.call-done = bf16[512,1024]{1,0:T(8,128)(2,1)} async-done(((bf16[128,1024]{1,0:T(8,128)(2,1)}), bf16[512,1024]{1,0:T(8,128)(2,1)}) %all-gather.5.cloned.1.call-update) | async-done | bytes 1048592 | tf_op jit(solution)/shard_map/all_gather | solution.py:72
  107.9 20.9 %all-gather.11.cloned.1.call-done = bf16[512,1024]{1,0:T(8,128)(2,1)} async-done(((bf16[128,1024]{1,0:T(8,128)(2,1)}), bf16[512,1024]{1,0:T(8,128)(2,1)}) %all-gather.11.cloned.1.call-update) | async-done | bytes 1048592 | tf_op jit(solution)/shard_map/all_gather | solution.py:72
  146.1 3.6 collective-permute-done.13
  156.0 5.7 %collective-permute-done.16 = bf16[136,1024]{1,0:T(8,128)(2,1)S(1)} collective-permute-done((bf16[136,1024]{1,0:T(8,128)(2,1)S(1)}, bf16[136,1024]{1,0:T(8,128)(2,1)S(1)}, u32[]{:S(2)}, u32[]{:S(2)}) %collective-permute-start.16) | collective-permute-done | bytes 278560 | tf_op jit(solution)/shard_map/ppermute | solution.py:19
  170.7 3.0 collective-permute-done.20
  179.5 3.7 fusion.16
  185.9 4.9 %collective-permute-start.25 = (bf16[136,1024]{1,0:T(8,128)(2,1)S(1)}, bf16[136,1024]{1,0:T(8,128)(2,1)S(1)}, u32[]{:S(2)}, u32[]{:S(2)}) collective-permute-start(bf16[136,1024]{1,0:T(8,128)(2,1)S(1)} %convolution_convert_fusion.7), channel_id=1, source_target_pairs={{0,20},{4,24},{8,28},{12,0},{16,4},{20,8},{24,12},{28,16},{1,21},{... | collective-permute-start | bytes 835592 | tf_op jit(solution)/shard_map/ppermute | solution.py:19
  190.8 6.3 %collective-permute-done.23 = bf16[136,1024]{1,0:T(8,128)(2,1)S(1)} collective-permute-done((bf16[136,1024]{1,0:T(8,128)(2,1)S(1)}, bf16[136,1024]{1,0:T(8,128)(2,1)S(1)}, u32[]{:S(2)}, u32[]{:S(2)}) %collective-permute-start.23) | collective-permute-done | bytes 278560 | tf_op jit(solution)/shard_map/ppermute | solution.py:19
  197.7 3.6 collective-permute-done.25
  201.3 6.6 %collective-permute-start.2 = (bf16[136,1024]{1,0:T(8,128)(2,1)S(1)}, bf16[136,1024]{1,0:T(8,128)(2,1)S(1)}, u32[]{:S(2)}, u32[]{:S(2)}) collective-permute-start(bf16[136,1024]{1,0:T(8,128)(2,1)S(1)} %copy-done.14), channel_id=1, source_target_pairs={{0,12},{4,16},{8,20},{12,24},{16,28},{20,0},{24,4},{28,8},{1,13},{... | collective-permute-start | bytes 835592 | tf_op jit(solution)/shard_map/ppermute | solution.py:19
  211.5 3.6 fusion.14
  218.7 5.4 %collective-permute-done.5 = bf16[136,1024]{1,0:T(8,128)(2,1)S(1)} collective-permute-done((bf16[136,1024]{1,0:T(8,128)(2,1)S(1)}, bf16[136,1024]{1,0:T(8,128)(2,1)S(1)}, u32[]{:S(2)}, u32[]{:S(2)}) %collective-permute-start.5) | collective-permute-done | bytes 278560 | tf_op jit(solution)/shard_map/ppermute | solution.py:19
  228.4 5.6 %multiply_convert_fusion = bf16[1088,768]{1,0:T(8,128)(2,1)S(1)} fusion(f32[1088,768]{1,0:T(8,128)S(1)} %fusion.1, f32[1088,768]{1,0:T(8,128)} %fusion.14, f32[1088,768]{1,0:T(8,128)} %fusion.16, f32[1088,768]{1,0:T(8,128)S(1)} %fusion.18, bf16[1088,1024]{1,0:T(8,128)(2,1)S(1)} %constant_dynamic-update-slice_fusion, bf16[1,4096,768]{2,1,0:T(8,128)(2,1)S(1)} %bitcast.131), kind=kOutput, calls=%fused_computation.10 | convolution fusion | flops 1718796288 | bytes 18841600 | tf_op jit(solution)/shard_map/dot_general | solution.py:11
  234.0 3.9 convolution_convert_fusion.3
  238.0 3.3 convolution_convert_fusion.2
  241.5 7.7 %collective-permute-start.28 = (bf16[136,1024]{1,0:T(8,128)(2,1)S(1)}, bf16[136,1024]{1,0:T(8,128)(2,1)S(1)}, u32[]{:S(2)}, u32[]{:S(2)}) collective-permute-start(bf16[136,1024]{1,0:T(8,128)(2,1)S(1)} %get-tuple-element.11), channel_id=1, source_target_pairs={{0,28},{4,0},{8,4},{12,8},{16,12},{20,16},{24,20},{28,24},{1,29},{... | collective-permute-start | bytes 835592 | tf_op jit(solution)/shard_map/ppermute | solution.py:19
  250.4 4.7 %convolution_convert_fusion.1 = bf16[1088,1024]{1,0:T(8,128)(2,1)} fusion(bf16[1088,768]{1,0:T(8,128)(2,1)S(1)} %multiply_convert_fusion, bf16[1,768,4096]{2,1,0:T(8,128)(2,1)} %param.17), kind=kOutput, calls=%fused_computation.7 | convolution fusion | flops 1712390144 | bytes 5472256 | tf_op jit(solution)/shard_map/dot_general | solution.py:11
  262.2 13.6 %collective-permute-done.31 = bf16[136,1024]{1,0:T(8,128)(2,1)S(1)} collective-permute-done((bf16[136,1024]{1,0:T(8,128)(2,1)S(1)}, bf16[136,1024]{1,0:T(8,128)(2,1)S(1)}, u32[]{:S(2)}, u32[]{:S(2)}) %collective-permute-start.31) | collective-permute-done | bytes 278560 | tf_op jit(solution)/shard_map/ppermute | solution.py:19
  275.8 3.8 collective-permute-done.32
  288.2 3.0 collective-permute-done.35
  291.2 5.9 %collective-permute-done.36 = bf16[136,1024]{1,0:T(8,128)(2,1)S(1)} collective-permute-done((bf16[136,1024]{1,0:T(8,128)(2,1)S(1)}, bf16[136,1024]{1,0:T(8,128)(2,1)S(1)}, u32[]{:S(2)}, u32[]{:S(2)}) %collective-permute-start.36) | collective-permute-done | bytes 278560 | tf_op jit(solution)/shard_map/ppermute | solution.py:19
  299.2 7.1 %collective-permute-start.42 = (bf16[136,1024]{1,0:T(8,128)(2,1)}, bf16[136,1024]{1,0:T(8,128)(2,1)}, u32[]{:S(2)}, u32[]{:S(2)}) collective-permute-start(bf16[136,1024]{1,0:T(8,128)(2,1)} %get-tuple-element.27), channel_id=1, source_target_pairs={{0,28},{4,0},{8,4},{12,8},{16,12},{20,16},{24,20},{28,24},{1,29},{... | collective-permute-start | bytes 835592 | tf_op jit(solution)/shard_map/ppermute | solution.py:19
  306.4 3.6 collective-permute-done.38
  316.8 5.4 %convolution_convert_fusion = bf16[1088,1024]{1,0:T(8,128)(2,1)} fusion(bf16[1088,768]{1,0:T(8,128)(2,1)} %copy-done.31, bf16[1,768,4096]{2,1,0:T(8,128)(2,1)} %param.17), kind=kOutput, calls=%fused_computation.6 | convolution fusion | flops 1712390144 | bytes 5472256 | tf_op jit(solution)/shard_map/dot_general | solution.py:11
  328.1 15.5 %collective-permute-done.45 = bf16[136,1024]{1,0:T(8,128)(2,1)S(1)} collective-permute-done((bf16[136,1024]{1,0:T(8,128)(2,1)S(1)}, bf16[136,1024]{1,0:T(8,128)(2,1)S(1)}, u32[]{:S(2)}, u32[]{:S(2)}) %collective-permute-start.45) | collective-permute-done | bytes 278560 | tf_op jit(solution)/shard_map/ppermute | solution.py:19
  355.1 3.9 collective-permute-done.49
  359.0 5.9 %collective-permute-done.50 = bf16[136,1024]{1,0:T(8,128)(2,1)S(1)} collective-permute-done((bf16[136,1024]{1,0:T(8,128)(2,1)S(1)}, bf16[136,1024]{1,0:T(8,128)(2,1)S(1)}, u32[]{:S(2)}, u32[]{:S(2)}) %collective-permute-start.50) | collective-permute-done | bytes 278560 | tf_op jit(solution)/shard_map/ppermute | solution.py:19
  367.0 12.4 %collective-permute-done.53 = bf16[136,1024]{1,0:T(8,128)(2,1)S(1)} collective-permute-done((bf16[136,1024]{1,0:T(8,128)(2,1)S(1)}, bf16[136,1024]{1,0:T(8,128)(2,1)S(1)}, u32[]{:S(2)}, u32[]{:S(2)}) %collective-permute-start.53) | collective-permute-done | bytes 278560 | tf_op jit(solution)/shard_map/ppermute | solution.py:19
  383.7 26.8 %reduce-scatter.11.cloned.1.call-done = bf16[128,1024]{1,0:T(8,128)(2,1)} async-done(((bf16[512,1024]{1,0:T(8,128)(2,1)}), bf16[128,1024]{1,0:T(8,128)(2,1)}) %reduce-scatter.11.cloned.1.call-update) | async-done | bytes 262160 | tf_op jit(solution)/shard_map/reduce_scatter | solution.py:89
  (314 shorter events, 147.8 us)
Async XLA Ops:
  6.5 35.1 %all-gather.7.cloned.1.call-start = ((), (), s32[]{:S(2)}) async-start(), calls=%async_computation.5 | async-start | bytes 1310720 | tf_op jit(solution)/shard_map/all_gather | solution.py:72
  10.7 60.2 %all-gather.9.cloned.1.call-start = ((), (), s32[]{:S(2)}) async-start(), calls=%async_computation.6 | async-start | bytes 1310720 | tf_op jit(solution)/shard_map/all_gather | solution.py:72
  11.4 88.5 %all-gather.5.cloned.1.call-start = ((), (), s32[]{:S(2)}) async-start(), calls=%async_computation.4 | async-start | bytes 1310720 | tf_op jit(solution)/shard_map/all_gather | solution.py:72
  12.2 116.6 %all-gather.11.cloned.1.call-start = ((), (), s32[]{:S(2)}) async-start(), calls=%async_computation.7 | async-start | bytes 1310720 | tf_op jit(solution)/shard_map/all_gather | solution.py:72
  12.7 370.9 %reduce-scatter.5.cloned.1.call-start = ((), (), s32[]{:S(2)}) async-start(), calls=%async_computation.8 | async-start | bytes 1310720 | tf_op jit(solution)/shard_map/reduce_scatter | solution.py:89
  44.0 90.3 %collective-permute-start.7 = (bf16[136,1024]{1,0:T(8,128)(2,1)}, bf16[136,1024]{1,0:T(8,128)(2,1)}, u32[]{:S(2)}, u32[]{:S(2)}) collective-permute-start(bf16[136,1024]{1,0:T(8,128)(2,1)} %convolution_convert_fusion.27), channel_id=1, source_target_pairs={{0,4},{4,8},{8,12},{12,16},{16,20},{20,24},{24,28},{28,0},{1,5},{5... | collective-permute-start | bytes 835592 | tf_op jit(solution)/shard_map/ppermute | solution.py:19
  46.3 91.4 %collective-permute-start.8 = (bf16[136,1024]{1,0:T(8,128)(2,1)}, bf16[136,1024]{1,0:T(8,128)(2,1)}, u32[]{:S(2)}, u32[]{:S(2)}) collective-permute-start(bf16[136,1024]{1,0:T(8,128)(2,1)} %convolution_convert_fusion.26), channel_id=1, source_target_pairs={{0,8},{4,12},{8,16},{12,20},{16,24},{20,28},{24,0},{28,4},{1,9},{5... | collective-permute-start | bytes 835592 | tf_op jit(solution)/shard_map/ppermute | solution.py:19
  48.8 90.2 %collective-permute-start.9 = (bf16[136,1024]{1,0:T(8,128)(2,1)}, bf16[136,1024]{1,0:T(8,128)(2,1)}, u32[]{:S(2)}, u32[]{:S(2)}) collective-permute-start(bf16[136,1024]{1,0:T(8,128)(2,1)} %convolution_convert_fusion.25), channel_id=1, source_target_pairs={{0,12},{4,16},{8,20},{12,24},{16,28},{20,0},{24,4},{28,8},{1,13},{... | collective-permute-start | bytes 835592 | tf_op jit(solution)/shard_map/ppermute | solution.py:19
  52.2 88.3 %collective-permute-start.10 = (bf16[136,1024]{1,0:T(8,128)(2,1)}, bf16[136,1024]{1,0:T(8,128)(2,1)}, u32[]{:S(2)}, u32[]{:S(2)}) collective-permute-start(bf16[136,1024]{1,0:T(8,128)(2,1)} %convolution_convert_fusion.24), channel_id=1, source_target_pairs={{0,16},{4,20},{8,24},{12,28},{16,0},{20,4},{24,8},{28,12},{1,17},{... | collective-permute-start | bytes 835592 | tf_op jit(solution)/shard_map/ppermute | solution.py:19
  53.8 88.3 %collective-permute-start.11 = (bf16[136,1024]{1,0:T(8,128)(2,1)}, bf16[136,1024]{1,0:T(8,128)(2,1)}, u32[]{:S(2)}, u32[]{:S(2)}) collective-permute-start(bf16[136,1024]{1,0:T(8,128)(2,1)} %convolution_convert_fusion.23), channel_id=1, source_target_pairs={{0,20},{4,24},{8,28},{12,0},{16,4},{20,8},{24,12},{28,16},{1,21},{... | collective-permute-start | bytes 835592 | tf_op jit(solution)/shard_map/ppermute | solution.py:19
  142.1 19.6 %collective-permute-start.16 = (bf16[136,1024]{1,0:T(8,128)(2,1)S(1)}, bf16[136,1024]{1,0:T(8,128)(2,1)S(1)}, u32[]{:S(2)}, u32[]{:S(2)}) collective-permute-start(bf16[136,1024]{1,0:T(8,128)(2,1)S(1)} %copy-done.21), channel_id=1, source_target_pairs={{0,12},{4,16},{8,20},{12,24},{16,28},{20,0},{24,4},{28,8},{1,13},{... | collective-permute-start | bytes 835592 | tf_op jit(solution)/shard_map/ppermute | solution.py:19
  144.6 19.0 %collective-permute-start.17 = (bf16[136,1024]{1,0:T(8,128)(2,1)S(1)}, bf16[136,1024]{1,0:T(8,128)(2,1)S(1)}, u32[]{:S(2)}, u32[]{:S(2)}) collective-permute-start(bf16[136,1024]{1,0:T(8,128)(2,1)S(1)} %copy-done.20), channel_id=1, source_target_pairs={{0,16},{4,20},{8,24},{12,28},{16,0},{20,4},{24,8},{28,12},{1,17},{... | collective-permute-start | bytes 835592 | tf_op jit(solution)/shard_map/ppermute | solution.py:19
  161.7 53.4 %collective-permute-start = (bf16[136,1024]{1,0:T(8,128)(2,1)S(1)}, bf16[136,1024]{1,0:T(8,128)(2,1)S(1)}, u32[]{:S(2)}, u32[]{:S(2)}) collective-permute-start(bf16[136,1024]{1,0:T(8,128)(2,1)S(1)} %copy-done.16), channel_id=1, source_target_pairs={{0,4},{4,8},{8,12},{12,16},{16,20},{20,24},{24,28},{28,0},{1,5},{5... | collective-permute-start | bytes 835592 | tf_op jit(solution)/shard_map/ppermute | solution.py:19
  163.5 52.8 %collective-permute-start.1 = (bf16[136,1024]{1,0:T(8,128)(2,1)S(1)}, bf16[136,1024]{1,0:T(8,128)(2,1)S(1)}, u32[]{:S(2)}, u32[]{:S(2)}) collective-permute-start(bf16[136,1024]{1,0:T(8,128)(2,1)S(1)} %copy-done.15), channel_id=1, source_target_pairs={{0,8},{4,12},{8,16},{12,20},{16,24},{20,28},{24,0},{28,4},{1,9},{5... | collective-permute-start | bytes 835592 | tf_op jit(solution)/shard_map/ppermute | solution.py:19
  167.0 17.8 %collective-permute-start.21 = (bf16[136,1024]{1,0:T(8,128)(2,1)S(1)}, bf16[136,1024]{1,0:T(8,128)(2,1)S(1)}, u32[]{:S(2)}, u32[]{:S(2)}) collective-permute-start(bf16[136,1024]{1,0:T(8,128)(2,1)S(1)} %convolution_convert_fusion.11), channel_id=1, source_target_pairs={{0,4},{4,8},{8,12},{12,16},{16,20},{20,24},{24,28},{28,0},{1,5},{5... | collective-permute-start | bytes 835592 | tf_op jit(solution)/shard_map/ppermute | solution.py:19
  173.7 23.5 %collective-permute-start.23 = (bf16[136,1024]{1,0:T(8,128)(2,1)S(1)}, bf16[136,1024]{1,0:T(8,128)(2,1)S(1)}, u32[]{:S(2)}, u32[]{:S(2)}) collective-permute-start(bf16[136,1024]{1,0:T(8,128)(2,1)S(1)} %convolution_convert_fusion.9), channel_id=1, source_target_pairs={{0,12},{4,16},{8,20},{12,24},{16,28},{20,0},{24,4},{28,8},{1,13},{... | collective-permute-start | bytes 835592 | tf_op jit(solution)/shard_map/ppermute | solution.py:19
  255.1 20.7 %collective-permute-start.31 = (bf16[136,1024]{1,0:T(8,128)(2,1)S(1)}, bf16[136,1024]{1,0:T(8,128)(2,1)S(1)}, u32[]{:S(2)}, u32[]{:S(2)}) collective-permute-start(bf16[136,1024]{1,0:T(8,128)(2,1)S(1)} %get-tuple-element.8), channel_id=1, source_target_pairs={{0,16},{4,20},{8,24},{12,28},{16,0},{20,4},{24,8},{28,12},{1,17},{... | collective-permute-start | bytes 835592 | tf_op jit(solution)/shard_map/ppermute | solution.py:19
  255.7 23.9 %collective-permute-start.32 = (bf16[136,1024]{1,0:T(8,128)(2,1)S(1)}, bf16[136,1024]{1,0:T(8,128)(2,1)S(1)}, u32[]{:S(2)}, u32[]{:S(2)}) collective-permute-start(bf16[136,1024]{1,0:T(8,128)(2,1)S(1)} %get-tuple-element.7), channel_id=1, source_target_pairs={{0,12},{4,16},{8,20},{12,24},{16,28},{20,0},{24,4},{28,8},{1,13},{... | collective-permute-start | bytes 835592 | tf_op jit(solution)/shard_map/ppermute | solution.py:19
  256.9 22.8 %collective-permute-start.33 = (bf16[136,1024]{1,0:T(8,128)(2,1)S(1)}, bf16[136,1024]{1,0:T(8,128)(2,1)S(1)}, u32[]{:S(2)}, u32[]{:S(2)}) collective-permute-start(bf16[136,1024]{1,0:T(8,128)(2,1)S(1)} %get-tuple-element.6), channel_id=1, source_target_pairs={{0,8},{4,12},{8,16},{12,20},{16,24},{20,28},{24,0},{28,4},{1,9},{5... | collective-permute-start | bytes 835592 | tf_op jit(solution)/shard_map/ppermute | solution.py:19
  283.8 99.9 %reduce-scatter.7.cloned.1.call-start = ((), (), s32[]{:S(2)}) async-start(), calls=%async_computation.9 | async-start | bytes 1310720 | tf_op jit(solution)/shard_map/reduce_scatter | solution.py:89
  284.9 25.1 %collective-permute-start.38 = (bf16[136,1024]{1,0:T(8,128)(2,1)S(1)}, bf16[136,1024]{1,0:T(8,128)(2,1)S(1)}, u32[]{:S(2)}, u32[]{:S(2)}) collective-permute-start(bf16[136,1024]{1,0:T(8,128)(2,1)S(1)} %get-tuple-element.16), channel_id=1, source_target_pairs={{0,16},{4,20},{8,24},{12,28},{16,0},{20,4},{24,8},{28,12},{1,17},{... | collective-permute-start | bytes 835592 | tf_op jit(solution)/shard_map/ppermute | solution.py:19
  286.3 26.2 %collective-permute-start.39 = (bf16[136,1024]{1,0:T(8,128)(2,1)S(1)}, bf16[136,1024]{1,0:T(8,128)(2,1)S(1)}, u32[]{:S(2)}, u32[]{:S(2)}) collective-permute-start(bf16[136,1024]{1,0:T(8,128)(2,1)S(1)} %get-tuple-element.15), channel_id=1, source_target_pairs={{0,12},{4,16},{8,20},{12,24},{16,28},{20,0},{24,4},{28,8},{1,13},{... | collective-permute-start | bytes 835592 | tf_op jit(solution)/shard_map/ppermute | solution.py:19
  291.2 21.3 %collective-permute-start.40 = (bf16[136,1024]{1,0:T(8,128)(2,1)S(1)}, bf16[136,1024]{1,0:T(8,128)(2,1)S(1)}, u32[]{:S(2)}, u32[]{:S(2)}) collective-permute-start(bf16[136,1024]{1,0:T(8,128)(2,1)S(1)} %get-tuple-element.14), channel_id=1, source_target_pairs={{0,8},{4,12},{8,16},{12,20},{16,24},{20,28},{24,0},{28,4},{1,9},{5... | collective-permute-start | bytes 835592 | tf_op jit(solution)/shard_map/ppermute | solution.py:19
  299.2 25.0 %collective-permute-start.42 = (bf16[136,1024]{1,0:T(8,128)(2,1)}, bf16[136,1024]{1,0:T(8,128)(2,1)}, u32[]{:S(2)}, u32[]{:S(2)}) collective-permute-start(bf16[136,1024]{1,0:T(8,128)(2,1)} %get-tuple-element.27), channel_id=1, source_target_pairs={{0,28},{4,0},{8,4},{12,8},{16,12},{20,16},{24,20},{28,24},{1,29},{... | collective-permute-start | bytes 835592 | tf_op jit(solution)/shard_map/ppermute | solution.py:19
  316.7 67.0 %reduce-scatter.9.cloned.1.call-start = ((), (), s32[]{:S(2)}) async-start(), calls=%async_computation.10 | async-start | bytes 1310720 | tf_op jit(solution)/shard_map/reduce_scatter | solution.py:89
  322.2 21.4 %collective-permute-start.45 = (bf16[136,1024]{1,0:T(8,128)(2,1)S(1)}, bf16[136,1024]{1,0:T(8,128)(2,1)S(1)}, u32[]{:S(2)}, u32[]{:S(2)}) collective-permute-start(bf16[136,1024]{1,0:T(8,128)(2,1)S(1)} %copy-done.13), channel_id=1, source_target_pairs={{0,16},{4,20},{8,24},{12,28},{16,0},{20,4},{24,8},{28,12},{1,17},{... | collective-permute-start | bytes 835592 | tf_op jit(solution)/shard_map/ppermute | solution.py:19
  322.7 23.0 %collective-permute-start.46 = (bf16[136,1024]{1,0:T(8,128)(2,1)S(1)}, bf16[136,1024]{1,0:T(8,128)(2,1)S(1)}, u32[]{:S(2)}, u32[]{:S(2)}) collective-permute-start(bf16[136,1024]{1,0:T(8,128)(2,1)S(1)} %copy-done.12), channel_id=1, source_target_pairs={{0,12},{4,16},{8,20},{12,24},{16,28},{20,0},{24,4},{28,8},{1,13},{... | collective-permute-start | bytes 835592 | tf_op jit(solution)/shard_map/ppermute | solution.py:19
  324.2 21.6 %collective-permute-start.47 = (bf16[136,1024]{1,0:T(8,128)(2,1)S(1)}, bf16[136,1024]{1,0:T(8,128)(2,1)S(1)}, u32[]{:S(2)}, u32[]{:S(2)}) collective-permute-start(bf16[136,1024]{1,0:T(8,128)(2,1)S(1)} %copy-done.11), channel_id=1, source_target_pairs={{0,8},{4,12},{8,16},{12,20},{16,24},{20,28},{24,0},{28,4},{1,9},{5... | collective-permute-start | bytes 835592 | tf_op jit(solution)/shard_map/ppermute | solution.py:19
  326.1 19.7 %collective-permute-start.48 = (bf16[136,1024]{1,0:T(8,128)(2,1)S(1)}, bf16[136,1024]{1,0:T(8,128)(2,1)S(1)}, u32[]{:S(2)}, u32[]{:S(2)}) collective-permute-start(bf16[136,1024]{1,0:T(8,128)(2,1)S(1)} %copy-done.10), channel_id=1, source_target_pairs={{0,4},{4,8},{8,12},{12,16},{16,20},{20,24},{24,28},{28,0},{1,5},{5... | collective-permute-start | bytes 835592 | tf_op jit(solution)/shard_map/ppermute | solution.py:19
  350.0 60.5 %reduce-scatter.11.cloned.1.call-start = ((), (), s32[]{:S(2)}) async-start(), calls=%async_computation.11 | async-start | bytes 1310720 | tf_op jit(solution)/shard_map/reduce_scatter | solution.py:89
  354.0 25.4 %collective-permute-start.53 = (bf16[136,1024]{1,0:T(8,128)(2,1)S(1)}, bf16[136,1024]{1,0:T(8,128)(2,1)S(1)}, u32[]{:S(2)}, u32[]{:S(2)}) collective-permute-start(bf16[136,1024]{1,0:T(8,128)(2,1)S(1)} %get-tuple-element.31), channel_id=1, source_target_pairs={{0,12},{4,16},{8,20},{12,24},{16,28},{20,0},{24,4},{28,8},{1,13},{... | collective-permute-start | bytes 835592 | tf_op jit(solution)/shard_map/ppermute | solution.py:19
  359.0 20.5 %collective-permute-start.54 = (bf16[136,1024]{1,0:T(8,128)(2,1)S(1)}, bf16[136,1024]{1,0:T(8,128)(2,1)S(1)}, u32[]{:S(2)}, u32[]{:S(2)}) collective-permute-start(bf16[136,1024]{1,0:T(8,128)(2,1)S(1)} %get-tuple-element.30), channel_id=1, source_target_pairs={{0,8},{4,12},{8,16},{12,20},{16,24},{20,28},{24,0},{28,4},{1,9},{5... | collective-permute-start | bytes 835592 | tf_op jit(solution)/shard_map/ppermute | solution.py:19
  (68 other events, 677.8 us)
Sparse Core Ops, SparseCore 0:
  10.8 30.8 all-gather.6
  43.2 27.6 all-gather.8
  72.5 27.4 all-gather.4
  101.3 27.4 all-gather.10
  283.9 26.1 reduce-scatter.4
  316.9 27.3 reduce-scatter.6
  350.1 26.6 reduce-scatter.8
  383.8 26.6 reduce-scatter.10
